TPU v7x, 32 devices: a whole 2x2x4 slice. The times are simulated.
32 devices in a mesh: groups: 2 (over x), space: 16 (over z, y, core).
Axes of the slice: x: 2, y: 2, z: 4, core: 2. Of those that a mesh axis runs over, the one named last changes fastest.
Arguments:
- probes: float32 [8, 40, 32768], P('groups', None, 'space'), parts along dimension 0
- prior_std: float32 [65536], P(('groups', 'space')), parts along dimension 0, may hold values from 0.4 to 2
- blocks: bfloat16 [9216, 128, 128], P(('groups', 'space')), parts along dimension 0, may hold values from -0.5 to 0.5
- footprint_block_scale: float32 [9216], P(('groups', 'space')), parts along dimension 0, may hold values from 0.1 to 1
- block_lists: int32 [9216, 3], P(('groups', 'space')), parts along dimension 0, may hold values from 0 to 39, as said below
- block_live: int32 [32], P(('groups', 'space')), parts along dimension 0, may hold values from 1 to 288, as said below
- noise_inv: float32 [4096], P('groups'), parts along dimension 0, may hold values from 0.2 to 1
- corr_days: float32 [2], P('groups'), parts along dimension 0, may hold values from 3 to 12
Outputs:
- hess_probes: float32 [8, 40, 32768], P('groups', None, 'space'), parts along dimension 0
- curvature: float32 [8], P('groups'), parts along dimension 0
There are 2 independent parts, one for each index of `groups`. A program takes and returns all parts, laid end to end along the dimension named above; each array names one. Nothing has to cross between parts.
Inputs may be any that keep to these rules, and one draw needn't show every extreme that they name: `block_lists`: column 0 lies in 0 to 15, column 1 in 0 to 15, column 2 in 0 to 39. `block_live`: some device has all 288 slots live in every draw.
All inputs are finite; a program needn't handle non-finite values.
Results may differ from a plain program's by a relative error of at most 0.0039.
Values may be sent and summed in bfloat16 or wider, within the bound.
A program may use at most 64 MiB of HBM per device.

v0:
```python
import jax
import jax.numpy as jnp
from jax import lax
from jax.sharding import PartitionSpec as P


def temporal_factor(corr_days, days):
    index = jnp.arange(days).astype(jnp.float32)
    corr = jnp.exp(-jnp.abs(index[:, None] - index[None, :]) / corr_days[0])
    return jnp.linalg.cholesky(corr)


def shards(
    probes, prior_std, blocks, footprint_block_scale, block_lists, block_live, noise_inv, corr_days
):
    count, days, cell_dev = probes.shape
    tiles = cell_dev // 128
    slots = blocks.shape[0]
    rec_blocks = noise_inv.shape[0] // 128
    factor = temporal_factor(corr_days, days)
    moved = jnp.einsum("ts,psc->ptc", factor, probes, precision=lax.Precision.HIGHEST)
    scaled = (moved * prior_std[None, None, :]).astype(jnp.bfloat16)
    grid = scaled.reshape(count, days * tiles, 128)
    slot_key = block_lists[:, 2] * tiles + block_lists[:, 1]
    weight = footprint_block_scale * (jnp.arange(slots) < block_live[0]).astype(jnp.float32)
    picked = jnp.take(grid, slot_key, axis=1)
    partial_value = jnp.einsum("pbc,brc->bpr", picked, blocks, preferred_element_type=jnp.float32)
    partial_value = partial_value * weight[:, None, None]
    obs = jax.ops.segment_sum(partial_value, block_lists[:, 0], num_segments=rec_blocks)
    inverse = noise_inv.reshape(rec_blocks, 128)
    total = lax.psum(obs, "space")
    resid = (total * inverse[:, None, :]).astype(jnp.bfloat16)
    fetched = jnp.take(resid, block_lists[:, 0], axis=0)
    contrib = jnp.einsum("bpr,brc->bpc", fetched, blocks, preferred_element_type=jnp.float32)
    contrib = contrib * weight[:, None, None]
    summed = jax.ops.segment_sum(contrib, slot_key, num_segments=days * tiles)
    summed = (
        summed.reshape(days, tiles, count, 128).transpose(2, 0, 1, 3).reshape(count, days, cell_dev)
    )
    back = summed * prior_std[None, None, :]
    hess_probes = probes + jnp.einsum("ts,ptc->psc", factor, back, precision=lax.Precision.HIGHEST)
    curvature = lax.psum(jnp.sum(probes * hess_probes, axis=(1, 2)), "space")
    return (hess_probes, curvature)


def solution(mesh):
    in_specs = (
        P("groups", None, "space"),
        P(("groups", "space")),
        P(("groups", "space"), None, None),
        P(("groups", "space")),
        P(("groups", "space"), None),
        P(("groups", "space")),
        P("groups"),
        P("groups"),
    )
    out_specs = (P("groups", None, "space"), P("groups"))
    return jax.shard_map(shards, mesh=mesh, in_specs=in_specs, out_specs=out_specs, check_vma=False)
```

profile of v0, /device:TPU:0, one launch (start us, length us, event | category | flops | bytes accessed | tf_op | source)
XLA Modules:
  0.0 151.8 jit_solution(2051734948561171767)
XLA Ops:
  1.9 0.7 fusion.20
  2.6 0.8 and_reduce_fusion
  3.5 0.7 fusion.27
  4.2 0.1 add_multiply_fusion
  4.3 3.6 %cholesky.18 = f32[40,40]{1,0:T(8,128)S(1)} custom-call(f32[40,40]{1,0:T(8,128)S(1)} %add_multiply_fusion), custom_call_target="Cholesky" | custom-call | tf_op jit(solution)/shard_map/jit(cholesky)/cholesky | solution.py:10
  8.0 0.6 compare_reduce_fusion
  8.6 3.2 %fusion.2 = bf16[4,40,2048]{2,1,0:T(8,128)(2,1)S(1)} fusion(f32[4,40,2048]{2,1,0:T(8,128)} %param.8, f32[2048]{0:T(1024)} %param.9, f32[40,40]{1,0:T(8,128)S(1)} %cholesky.18, pred[]{:T(512)} %compare_reduce_fusion), kind=kOutput, calls=%fused_computation.8 | convolution fusion | flops 157946560 | bytes 1980673 | tf_op jit(solution)/shard_map/ts,psc->ptc/dot_general | solution.py:21
  11.8 0.3 reshape.38
  12.1 0.5 copy.11
  12.6 2.1 %gather_fusion = bf16[288,4,128]{2,1,0:T(4,128)(2,1)S(1)} fusion(bf16[4,640,128]{2,0,1:T(4,128)(2,1)S(1)} %copy.11, s32[1024]{0:T(1024)S(1)} %pad_clamp_fusion.1), kind=kCustom, calls=%fused_computation | custom fusion | bytes 590976 | tf_op jit(solution)/shard_map/jit(_take)/gather | solution.py:26
  14.8 8.1 %convolution_multiply_fusion.2 = f32[288,4,128]{2,1,0:T(4,128)S(1)} fusion(bf16[288,128,128]{2,1,0:T(8,128)(2,1)} %param.10, bf16[288,4,128]{2,1,0:T(4,128)(2,1)S(1)} %gather_fusion, f32[288]{0:T(512)S(1)} %fusion.20, pred[288]{0:T(512)(128)(4,1)S(1)} %get-tuple-element.6), kind=kOutput, calls=%fused_computation.12 | convolution fusion | flops 38043648 | bytes 10323360 | tf_op jit(solution)/shard_map/pbc,brc->bpr/dot_general | solution.py:27
  22.9 0.0 copy-start.2
  22.9 11.0 %scatter_fusion = f32[16,4,128]{2,1,0:T(4,128)S(1)} fusion(f32[16,4,128]{2,1,0:T(4,128)S(1)} %broadcast_in_dim.37, s32[288]{0:T(512)S(1)} %get-tuple-element.11, f32[288,4,128]{2,1,0:T(4,128)S(1)} %convolution_multiply_fusion.2), kind=kCustom, calls=%fused_computation.2 | custom fusion | flops 147456 | bytes 1770624 | tf_op jit(solution)/shard_map/scatter-add | solution.py:29
  34.0 63.0 %psum.14 = f32[16,4,128]{2,1,0:T(4,128)S(1)} all-reduce(f32[16,4,128]{2,1,0:T(4,128)S(1)} %scatter_fusion), channel_id=1, replica_groups=mesh['groups'=2,'space'=16] {'space'}, use_global_device_ids=true, to_apply=%region_3.4 | all-reduce | flops 8192 | bytes 65536 | tf_op jit(solution)/shard_map/psum | solution.py:31
  96.9 0.0 copy-done.2
  96.9 2.1 %gather_fusion.1 = bf16[288,4,128]{2,1,0:T(4,128)(2,1)S(1)} fusion(bf16[16,4,128]{2,1,0:T(4,128)(2,1)S(1)} %multiply_convert_fusion, s32[1024]{0:T(1024)S(1)} %pad_clamp_fusion), kind=kCustom, calls=%fused_computation.1 | custom fusion | bytes 590976 | tf_op jit(solution)/shard_map/jit(_take)/gather | solution.py:33
  99.1 5.8 %convolution_multiply_fusion.1 = f32[288,4,128]{2,1,0:T(4,128)S(1)} fusion(bf16[288,128,128]{2,1,0:T(8,128)(2,1)} %param.10, bf16[288,4,128]{2,1,0:T(4,128)(2,1)S(1)} %gather_fusion.1, f32[288]{0:T(512)S(1)} %fusion.20, pred[288]{0:T(512)(128)(4,1)S(1)} %get-tuple-element.8), kind=kOutput, calls=%fused_computation.11 | convolution fusion | flops 38043648 | bytes 10323360 | tf_op jit(solution)/shard_map/bpr,brc->bpc/dot_general | solution.py:34
  104.8 0.2 broadcast_in_dim.35
  105.0 10.8 %scatter_fusion.1 = f32[640,4,128]{2,1,0:T(4,128)S(1)} fusion(f32[640,4,128]{2,1,0:T(4,128)S(1)} %broadcast_in_dim.35, s32[288]{0:T(512)S(1)} %get-tuple-element.5, f32[288,4,128]{2,1,0:T(4,128)S(1)} %convolution_multiply_fusion.1), kind=kCustom, calls=%fused_computation.3 | custom fusion | flops 147456 | bytes 1770624 | tf_op jit(solution)/shard_map/scatter-add | solution.py:36
  115.8 1.2 copy.12
  117.0 0.0 copy-start
  117.0 0.0 copy-start.1
  117.0 1.6 %reshape.40 = f32[4,40,2048]{2,1,0:T(8,128)S(1)} reshape(f32[4,40,16,128]{3,2,1,0:T(8,128)} %copy.12) | data formatting | bytes 2621440 | tf_op jit(solution)/shard_map/reshape | solution.py:38
  118.6 0.1 copy-done
  118.7 0.0 copy-done.1
  118.7 3.1 %multiply_reduce_fusion = (f32[4]{0:T(128)S(1)}, f32[4,40,2048]{2,1,0:T(8,128)}) fusion(f32[4,40,2048]{2,1,0:T(8,128)S(1)} %copy-done, f32[40,40]{1,0:T(8,128)S(1)} %cholesky.18, pred[]{:T(512)} %compare_reduce_fusion, f32[4,40,2048]{2,1,0:T(8,128)S(1)} %reshape.40, f32[2048]{0:T(1024)S(1)} %copy-done.1), kind=kOutput, calls=%fused_computation.9 | convolution fusion | flops 158601920 | bytes 3946769 | tf_op jit(solution)/shard_map/ts,ptc->psc/dot_general | solution.py:41
  121.8 30.0 %psum.15 = f32[4]{0:T(128)} all-reduce(f32[4]{0:T(128)S(1)} %get-tuple-element.9), channel_id=1, replica_groups=mesh['groups'=2,'space'=16] {'space'}, use_global_device_ids=true, to_apply=%region_6.7 | all-reduce | flops 4 | bytes 32 | tf_op jit(solution)/shard_map/psum | solution.py:42
  (6 shorter events, 0.1 us)
Async XLA Ops:
  22.9 74.1 %copy-start.2 = (f32[2048]{0:T(1024)S(1)}, f32[2048]{0:T(1024)}, u32[]{:S(2)}) copy-start(f32[2048]{0:T(1024)} %param.14) | copy-start | bytes 24580
  117.0 1.7 %copy-start = (f32[4,40,2048]{2,1,0:T(8,128)S(1)}, f32[4,40,2048]{2,1,0:T(8,128)}, u32[]{:S(2)}) copy-start(f32[4,40,2048]{2,1,0:T(8,128)} %param.8) | copy-start | bytes 3932164
  117.0 1.7 %copy-start.1 = (f32[2048]{0:T(1024)S(1)}, f32[2048]{0:T(1024)}, u32[]{:S(2)}) copy-start(f32[2048]{0:T(1024)} %param.9) | copy-start | bytes 24580
where the time goes:
time: 152 us
  blocking collectives  92.9 us (61%)
  other arithmetic  28.5 us (19%)
  matrix products  20.1 us (13%)
  local copies, waits for them, and re-layouts  8.16 us (5%)
  between operations  2.05 us (1%)
    psum x1, blocking collectives, shards(): total = lax.psum(obs, 'space')  63 us
    psum x1, blocking collectives, shards(): curvature = lax.psum(jnp.sum(probes * hess_probes, axis=(1, 2)), 'space')  30 us
    scatter-add x1, other arithmetic, shards(): jax.ops.segment_sum(partial_value, block_lists[:, 0], num_segments=rec_bl...  11 us
    scatter-add x1, other arithmetic, shards(): summed = jax.ops.segment_sum(contrib, slot_key, num_segments=days * tiles)  10.8 us
    dot_general x1, matrix products, shards(): jnp.einsum('pbc,brc->bpr', picked, blocks, preferred_element_type=jnp.flo...  8.12 us
    dot_general x1, matrix products, shards(): jnp.einsum('bpr,brc->bpc', fetched, blocks, preferred_element_type=jnp.fl...  5.75 us
    another operation x3, other arithmetic, temporal_factor(): return jnp.linalg.cholesky(corr)  4.32 us
    dot_general x1, matrix products, shards(): jnp.einsum('ts,psc->ptc', factor, probes, precision=lax.Precision.HIGHEST)  3.16 us

commit v1 on v0

v1 whole, which is shorter than its diff:
```python
import functools

import jax
import jax.numpy as jnp
from jax import lax
from jax.experimental import pallas as pl
from jax.experimental.pallas import tpu as pltpu
from jax.sharding import PartitionSpec as P

MESH = pl.DeviceIdType.MESH
CHUNKS = 8
PAD = 8


def split(x):
    high = x.astype(jnp.bfloat16)
    return high, (x - high.astype(jnp.float32)).astype(jnp.bfloat16)


def mm(a, b):
    return jnp.dot(a, b, preferred_element_type=jnp.float32)


def kernel(
    n,
    lists_s,
    live_s,
    corr_ref,
    lists_v,
    scale_ref,
    prior_ref,
    noise_ref,
    probes_hbm,
    blocks_hbm,
    hess_ref,
    curv_ref,
    x_buf,
    b_buf,
    s_buf,
    parts,
    res_buf,
    spread,
    snd,
    rc1,
    gat,
    x_sem,
    b_sem,
    send1,
    recv1,
    send2,
    recv2,
):
    rows, cells = x_buf.shape
    count = 4
    days = rows // count
    tiles = cells // 128
    slots = lists_v.shape[1]
    rec = noise_ref.shape[0]
    own = rec // n
    per = slots // CHUNKS
    f32 = jnp.float32
    me = lax.axis_index("space")

    x_copy = pltpu.make_async_copy(probes_hbm, x_buf, x_sem)
    x_copy.start()
    b_copies = []
    for c in range(CHUNKS):
        part = pl.ds(c * per * 128, per * 128)
        cp = pltpu.make_async_copy(blocks_hbm.at[part], b_buf.at[part], b_sem.at[c])
        cp.start()
        b_copies.append(cp)

    barrier = pltpu.get_barrier_semaphore()

    @pl.loop(1, n)
    def _(o):
        pl.semaphore_signal(
            barrier, inc=1, device_id={"space": lax.rem(me + o, n)}, device_id_type=MESH
        )

    rate = -1.0 / corr_ref[...]
    rest = jnp.sqrt(1.0 - jnp.exp(2.0 * rate))

    row = lax.broadcasted_iota(jnp.int32, (rows, 1), 0)
    col = lax.broadcasted_iota(jnp.int32, (1, rows), 1)
    row_t, row_p = row // count, row % count
    col_p = sum((col >= days * p).astype(jnp.int32) for p in range(1, count))
    col_s = col - days * col_p
    lag = row_t - col_s
    value = jnp.exp(rate * lag.astype(f32)) * jnp.where(col_s == 0, 1.0, rest)
    factor = jnp.where((lag >= 0) & (row_p == col_p), value, 0.0)
    f_hi, f_lo = split(factor)

    r_k, j_k, t_k = lists_v[0:1, :], lists_v[1:2, :], lists_v[2:3, :]
    lane = lax.broadcasted_iota(jnp.int32, (1, slots), 1)
    weight = jnp.where(lane < live_s[0], scale_ref[...], 0.0)

    s_buf[0:PAD, :] = jnp.zeros((PAD, 128), f32)
    s_buf[PAD + tiles * rows :, :] = jnp.zeros((PAD, 128), f32)
    res_buf[0:PAD, :] = jnp.zeros((PAD, 128), f32)
    res_buf[PAD + rec * count :, :] = jnp.zeros((PAD, 128), f32)

    x_copy.wait()
    square = jnp.zeros((rows, 128), f32)
    for j in range(0, tiles, 2):
        x = x_buf[:, j * 128 : j * 128 + 256]
        square = square + x[:, :128] * x[:, :128] + x[:, 128:] * x[:, 128:]
        x_hi, x_lo = split(x)
        moved = mm(f_hi, x_hi) + mm(f_hi, x_lo) + mm(f_lo, x_hi)
        scaled = (moved * prior_ref[:, j * 128 : j * 128 + 256]).astype(jnp.bfloat16).astype(f32)
        s_buf[PAD + j * rows : PAD + (j + 1) * rows, :] = scaled[:, :128]
        s_buf[PAD + (j + 1) * rows : PAD + (j + 2) * rows, :] = scaled[:, 128:]
    norm = jnp.sum(square.reshape(count, days, 128), axis=1)
    norm = jnp.concatenate([jnp.zeros_like(norm), norm], axis=0)

    low = lax.broadcasted_iota(jnp.int32, (8, 128), 0) < 4

    def forward(q, carry):
        k = q * 4

        def at(i):
            return PAD + lists_s[1, k + i] * rows + lists_s[2, k + i] * count

        a = jnp.where(low, s_buf[pl.ds(at(0), 8), :], s_buf[pl.ds(at(1) - 4, 8), :])
        b = jnp.where(low, s_buf[pl.ds(at(2), 8), :], s_buf[pl.ds(at(3) - 4, 8), :])
        lhs = jnp.concatenate([a, b], axis=0).astype(jnp.bfloat16)
        rhs = b_buf[pl.ds(pl.multiple_of(q * 512, 512), 512), :]
        o = lax.dot_general(lhs, rhs, (((1,), (1,)), ((), ())), preferred_element_type=f32)
        top = jnp.where(low, o[0:8, 0:128], o[0:8, 128:256])
        bot = jnp.where(low, o[8:16, 256:384], o[8:16, 384:512])
        parts[pl.ds(pl.multiple_of(q * 16, 16), 16), :] = jnp.concatenate([top, bot], axis=0)
        return carry

    quads = per // 4
    for c in range(CHUNKS):
        b_copies[c].wait()
        lax.fori_loop(c * quads, (c + 1) * quads, forward, 0, unroll=3)

    srow = lax.broadcasted_iota(jnp.int32, (rec * 8, 1), 0)
    pick = jnp.where(srow // 8 == r_k, weight, 0.0)
    obs = jnp.zeros((rec * 8, 128), f32)
    for p in range(count):
        h_hi, h_lo = split(jnp.where(srow % 8 == p, pick, 0.0))
        v_hi, v_lo = split(parts[pl.ds(p, slots, stride=count), :])
        obs = obs + mm(h_hi, v_hi) + mm(h_hi, v_lo) + mm(h_lo, v_hi)
    snd[...] = (obs.reshape(rec, 8, 128) + norm[None]).reshape(n, own, 8, 128)

    pl.semaphore_wait(barrier, n - 1)

    def first(o):
        peer = lax.rem(me + o, n)
        return pltpu.make_async_remote_copy(
            src_ref=snd.at[peer],
            dst_ref=rc1.at[me],
            send_sem=send1.at[peer],
            recv_sem=recv1.at[me],
            device_id={"space": peer},
            device_id_type=MESH,
        )

    def second(o):
        peer = lax.rem(me + o, n)
        return pltpu.make_async_remote_copy(
            src_ref=gat.at[me],
            dst_ref=gat.at[me],
            send_sem=send2.at[peer],
            recv_sem=recv2.at[me],
            device_id={"space": peer},
            device_id_type=MESH,
        )

    def arrived(buf, sem, o):
        peer = lax.rem(me + o, n)
        return pltpu.make_async_remote_copy(
            src_ref=buf.at[peer],
            dst_ref=buf.at[peer],
            send_sem=sem.at[peer],
            recv_sem=sem.at[peer],
            device_id={"space": peer},
            device_id_type=MESH,
        )

    @pl.loop(1, n)
    def _(o):
        first(o).start()

    rc1[me] = snd[me]

    day = lax.broadcasted_iota(jnp.int32, (days, 1), 0)
    late = t_k - day
    grow = jnp.exp(rate * late.astype(f32)) * jnp.where(day == 0, 1.0, rest)
    grow = jnp.where(late >= 0, grow, 0.0) * weight
    for j in range(tiles):
        spread[j * days : (j + 1) * days, :] = jnp.where(j_k == j, grow, 0.0)

    @pl.loop(1, n)
    def _(o):
        arrived(rc1, recv1, o).wait_recv()

    gat[me] = jnp.sum(rc1[...], axis=0)

    @pl.loop(1, n)
    def _(o):
        second(o).start()

    @pl.loop(1, n)
    def _(o):
        first(o).wait_send()

    @pl.loop(1, n)
    def _(o):
        arrived(gat, recv2, o).wait_recv()

    total = gat[...].reshape(rec, 8, 128)
    resid = (total * noise_ref[...][:, None, :]).astype(jnp.bfloat16).astype(f32)
    for r in range(rec):
        res_buf[PAD + r * count : PAD + (r + 1) * count, :] = resid[r, :count, :]
    energy = jnp.sum(total * resid, axis=0)
    energy = energy[:count] + total[0, count:]
    curv_ref[...] = jnp.broadcast_to(jnp.sum(energy, axis=1, keepdims=True), (count, 128))

    def backward(q, carry):
        k = q * 4

        def at(i):
            return PAD + lists_s[0, k + i] * count

        outs = []
        for h in range(2):
            a = jnp.where(low, res_buf[pl.ds(at(2 * h), 8), :], 0.0)
            b = jnp.where(low, 0.0, res_buf[pl.ds(at(2 * h + 1) - 4, 8), :])
            lhs = jnp.concatenate([a, b], axis=1).astype(jnp.bfloat16)
            rhs = b_buf[pl.ds(pl.multiple_of(q * 512 + h * 256, 256), 256), :]
            outs.append(mm(lhs, rhs))
        parts[pl.ds(pl.multiple_of(q * 16, 16), 16), :] = jnp.concatenate(outs, axis=0)
        return carry

    lax.fori_loop(0, slots // 4, backward, 0, unroll=4)

    g_hi = spread[...].astype(jnp.bfloat16)
    for p in range(count):
        v_hi = parts[pl.ds(p, slots, stride=count), :].astype(jnp.bfloat16)
        image = mm(g_hi, v_hi)
        for j in range(tiles):
            here = (slice(p * days, (p + 1) * days), slice(j * 128, (j + 1) * 128))
            back = image[j * days : (j + 1) * days, :] * prior_ref[:, j * 128 : (j + 1) * 128]
            hess_ref[here] = x_buf[here] + back

    @pl.loop(1, n)
    def _(o):
        second(o).wait_send()


def shards(
    n, probes, prior_std, blocks, footprint_block_scale, block_lists, block_live, noise_inv, corr_days
):
    count, days, cells = probes.shape
    slots = blocks.shape[0]
    rec = noise_inv.shape[0] // 128
    rows = count * days
    tiles = cells // 128
    own = rec // n
    lists = block_lists.T
    vmem = pl.BlockSpec(memory_space=pltpu.VMEM)
    smem = pl.BlockSpec(memory_space=pltpu.SMEM)
    hbm = pl.BlockSpec(memory_space=pl.ANY)
    dma = pltpu.SemaphoreType.DMA
    hess, curv = pl.pallas_call(
        functools.partial(kernel, n),
        out_shape=(
            jax.ShapeDtypeStruct((rows, cells), jnp.float32),
            jax.ShapeDtypeStruct((count, 128), jnp.float32),
        ),
        in_specs=[smem, smem, vmem, vmem, vmem, vmem, vmem, hbm, hbm],
        out_specs=(vmem, vmem),
        scratch_shapes=[
            pltpu.VMEM((rows, cells), jnp.float32),
            pltpu.VMEM((slots * 128, 128), jnp.bfloat16),
            pltpu.VMEM((tiles * rows + 2 * PAD, 128), jnp.float32),
            pltpu.VMEM((slots * count, 128), jnp.float32),
            pltpu.VMEM((rec * count + 2 * PAD, 128), jnp.float32),
            pltpu.VMEM((tiles * days, slots), jnp.float32),
            pltpu.VMEM((n, own, 8, 128), jnp.float32),
            pltpu.VMEM((n, own, 8, 128), jnp.float32),
            pltpu.VMEM((n, own, 8, 128), jnp.float32),
            dma(()),
            dma((CHUNKS,)),
            dma((n,)),
            dma((n,)),
            dma((n,)),
            dma((n,)),
        ],
        compiler_params=pltpu.CompilerParams(
            collective_id=0, has_side_effects=True, vmem_limit_bytes=48 * 1024 * 1024
        ),
    )(
        lists,
        block_live,
        corr_days.reshape(1, 1),
        lists,
        footprint_block_scale.reshape(1, slots),
        prior_std.reshape(1, cells),
        noise_inv.reshape(rec, 128),
        probes.reshape(rows, cells),
        blocks.reshape(slots * 128, 128),
    )
    return hess.reshape(count, days, cells), curv[:, 0]


def solution(mesh):
    in_specs = (
        P("groups", None, "space"),
        P(("groups", "space")),
        P(("groups", "space"), None, None),
        P(("groups", "space")),
        P(("groups", "space"), None),
        P(("groups", "space")),
        P("groups"),
        P("groups"),
    )
    out_specs = (P("groups", None, "space"), P("groups"))
    return jax.shard_map(
        functools.partial(shards, mesh.shape["space"]),
        mesh=mesh,
        in_specs=in_specs,
        out_specs=out_specs,
        check_vma=False,
    )
```

time: 152 us -> 31.3 us (0.21)
  blocking collectives: 92.9 us -> 0 us
  other arithmetic: 28.5 us -> 0 us
  Pallas kernels: 0 us -> 23.3 us
  matrix products: 20.1 us -> 0 us
  local copies, waits for them, and re-layouts: 8.16 us -> 5.77 us
    psum x2 -> x0, blocking collectives: 92.9 us -> none  [the longest x1 63 us: shards(): total = lax.psum(obs, 'space')]
    pallas_call x0 -> x1, Pallas kernels: none -> 23.3 us  [shards(): pl.pallas_call(functools.partial(kernel, n), out_shape=(jax.ShapeDtypeStr...]
    scatter-add x2 -> x0, other arithmetic: 21.9 us -> none  [the longest x1 11 us: shards(): jax.ops.segment_sum(partial_value, block_lists[:, 0], num_segments=rec_bl...]
    dot_general x4 -> x0, matrix products: 20.1 us -> none  [the longest x1 8.12 us: shards(): jnp.einsum('pbc,brc->bpr', picked, blocks, preferred_element_type=jnp.flo...]
    unnamed x6 -> x9, local copies, waits for them, and re-layouts: 0.13 us -> 4.46 us
    another operation x3 -> x0, other arithmetic: 4.32 us -> none  [temporal_factor(): return jnp.linalg.cholesky(corr)]
    gather x2 -> x0, local copies, waits for them, and re-layouts: 4.29 us -> none  [the longest x1 2.14 us: shards(): fetched = jnp.take(resid, block_lists[:, 0], axis=0)]
    reshape x3 -> x1, local copies, waits for them, and re-layouts: 2.39 us -> 0.68 us  [shards(): footprint_block_scale.reshape(1, slots)]
where the time goes in v1:
time: 31.3 us; the launch traced here: 31 us
  Pallas kernels  23.3 us (74%)
  local copies, waits for them, and re-layouts  5.77 us (18%)
  between operations  1.94 us (6%)
    pallas_call x1, Pallas kernels, shards(): pl.pallas_call(functools.partial(kernel, n), out_shape=(jax.ShapeDtypeStr...  23.3 us
    unnamed x9, local copies, waits for them, and re-layouts  4.46 us
    reshape x1, local copies, waits for them, and re-layouts, shards(): footprint_block_scale.reshape(1, slots)  0.68 us
    slice x1, local copies, waits for them, and re-layouts, shards(): return (hess.reshape(count, days, cells), curv[:, 0])  0.63 us

profile of v1, /device:TPU:0, one launch (start us, length us, event | category | flops | bytes accessed | tf_op | source)
XLA Modules:
  0.0 31.0 jit_solution(11432434304447563274)
XLA Ops:
  1.9 0.7 %reshape.26.scale_ref = f32[1,288]{1,0:T(1,128)S(1)} reshape(f32[288]{0:T(512)} %param.11) | data formatting | bytes 2304 | tf_op jit(solution)/shard_map/reshape | solution.py:301
  2.6 0.0 copy-start
  2.6 1.3 %copy-done = f32[4,40,2048]{2,1,0:T(8,128)S(1)} copy-done((f32[4,40,2048]{2,1,0:T(8,128)S(1)}, f32[4,40,2048]{2,1,0:T(8,128)}, u32[]{:S(2)}) %copy-start) | copy-done | bytes 1310744
  3.9 0.0 copy-start.1
  3.9 0.7 %copy-done.1 = s32[288,3]{0,1:T(4,128)S(1)} copy-done((s32[288,3]{0,1:T(4,128)S(1)}, s32[288,3]{0,1:T(4,128)}, u32[]{:S(2)}) %copy-start.1) | copy-done | bytes 3480
  4.6 0.0 copy-start.2
  4.6 0.7 %copy-done.2 = f32[2048]{0:T(1024)S(1)} copy-done((f32[2048]{0:T(1024)S(1)}, f32[2048]{0:T(1024)}, u32[]{:S(2)}) %copy-start.2) | copy-done | bytes 8216
  5.3 0.0 copy-start.3
  5.3 0.7 %copy-done.3 = f32[2048]{0:T(1024)S(1)} copy-done((f32[2048]{0:T(1024)S(1)}, f32[2048]{0:T(1024)}, u32[]{:S(2)}) %copy-start.3) | copy-done | bytes 8216
  6.0 23.3 %shard_map.95 = (f32[160,2048]{1,0:T(8,128)S(1)}, f32[4,128]{1,0:T(4,128)S(1)}) custom-call(s32[3,288]{1,0:T(4,128)S(1)} %bitcast.10, s32[1]{0:T(128)S(6)} %copy.11.live_s, f32[1,1]{1,0:T(1,128)} %bitcast.7.corr_ref, s32[3,288]{1,0:T(4,128)S(1)} %bitcast.11, f32[1,288]{1,0:T(1,128)S(1)} %reshape.26.scale_ref, f32[1,2048]{1,0:T(1,128)S(1)} %bitcast.12, ...), custom_call_target="tpu_custom_call" | custom-call | tf_op jit(solution)/shard_map/pallas_call | solution.py:268
  29.3 0.6 %slice_reduce_fusion = f32[4]{0:T(128)} fusion(f32[4,128]{1,0:T(4,128)S(1)} %get-tuple-element.5), kind=kLoop, calls=%fused_computation | loop fusion | bytes 32 | tf_op jit(solution)/shard_map/slice | solution.py:307
  29.9 1.1 %copy.13 = f32[4,40,2048]{2,1,0:T(8,128)} copy(f32[4,40,2048]{2,1,0:T(8,128)S(1)} %bitcast.9) | data formatting | bytes 2621440
Async XLA Ops:
  2.6 1.3 %copy-start = (f32[4,40,2048]{2,1,0:T(8,128)S(1)}, f32[4,40,2048]{2,1,0:T(8,128)}, u32[]{:S(2)}) copy-start(f32[4,40,2048]{2,1,0:T(8,128)} %param.8) | copy-start | bytes 3932164
  3.9 0.7 %copy-start.1 = (s32[288,3]{0,1:T(4,128)S(1)}, s32[288,3]{0,1:T(4,128)}, u32[]{:S(2)}) copy-start(s32[288,3]{0,1:T(4,128)} %param.12) | copy-start | bytes 10372
  4.6 0.7 %copy-start.2 = (f32[2048]{0:T(1024)S(1)}, f32[2048]{0:T(1024)}, u32[]{:S(2)}) copy-start(f32[2048]{0:T(1024)} %param.9) | copy-start | bytes 24580
  5.3 0.7 %copy-start.3 = (f32[2048]{0:T(1024)S(1)}, f32[2048]{0:T(1024)}, u32[]{:S(2)}) copy-start(f32[2048]{0:T(1024)} %param.14) | copy-start | bytes 24580

commit v2 on v1

--- a/solution.py
+++ b/solution.py
@@ -10,6 +10,11 @@
 MESH = pl.DeviceIdType.MESH
 CHUNKS = 8
 PAD = 8
+LIMIT = 48 * 1024 * 1024
+
+
+def hold(x):
+    return pltpu.with_memory_space_constraint(x, pltpu.HBM)
 
 
 def split(x):
@@ -23,17 +28,21 @@
 
 def kernel(
     n,
+    live_s,
+    corr_s,
+    lists_hbm,
+    scale_hbm,
+    prior_hbm,
+    noise_hbm,
+    probes_hbm,
+    blocks_hbm,
+    hess_ref,
+    curv_ref,
     lists_s,
-    live_s,
-    corr_ref,
     lists_v,
     scale_ref,
     prior_ref,
     noise_ref,
-    probes_hbm,
-    blocks_hbm,
-    hess_ref,
-    curv_ref,
     x_buf,
     b_buf,
     s_buf,
@@ -43,7 +52,7 @@
     snd,
     rc1,
     gat,
-    x_sem,
+    in_sem,
     b_sem,
     send1,
     recv1,
@@ -61,8 +70,21 @@
     f32 = jnp.float32
     me = lax.axis_index("space")
 
-    x_copy = pltpu.make_async_copy(probes_hbm, x_buf, x_sem)
+    x_copy = pltpu.make_async_copy(probes_hbm, x_buf, in_sem.at[0])
     x_copy.start()
+    small = []
+    for i, (src, dst) in enumerate(
+        (
+            (lists_hbm, lists_s),
+            (lists_hbm, lists_v),
+            (scale_hbm, scale_ref),
+            (prior_hbm, prior_ref),
+            (noise_hbm, noise_ref),
+        )
+    ):
+        cp = pltpu.make_async_copy(src, dst, in_sem.at[i + 1])
+        cp.start()
+        small.append(cp)
     b_copies = []
     for c in range(CHUNKS):
         part = pl.ds(c * per * 128, per * 128)
@@ -78,7 +100,7 @@
             barrier, inc=1, device_id={"space": lax.rem(me + o, n)}, device_id_type=MESH
         )
 
-    rate = -1.0 / corr_ref[...]
+    rate = -1.0 / jnp.full((1, 1), corr_s[0], f32)
     rest = jnp.sqrt(1.0 - jnp.exp(2.0 * rate))
 
     row = lax.broadcasted_iota(jnp.int32, (rows, 1), 0)
@@ -91,9 +113,12 @@
     factor = jnp.where((lag >= 0) & (row_p == col_p), value, 0.0)
     f_hi, f_lo = split(factor)
 
+    for cp in small:
+        cp.wait()
+
     r_k, j_k, t_k = lists_v[0:1, :], lists_v[1:2, :], lists_v[2:3, :]
     lane = lax.broadcasted_iota(jnp.int32, (1, slots), 1)
-    weight = jnp.where(lane < live_s[0], scale_ref[...], 0.0)
+    weight = jnp.where(lane < live_s[0], scale_ref[...].reshape(1, slots), 0.0)
 
     s_buf[0:PAD, :] = jnp.zeros((PAD, 128), f32)
     s_buf[PAD + tiles * rows :, :] = jnp.zeros((PAD, 128), f32)
@@ -134,7 +159,7 @@
     quads = per // 4
     for c in range(CHUNKS):
         b_copies[c].wait()
-        lax.fori_loop(c * quads, (c + 1) * quads, forward, 0, unroll=3)
+        lax.fori_loop(c * quads, (c + 1) * quads, forward, 0, unroll=9)
 
     srow = lax.broadcasted_iota(jnp.int32, (rec * 8, 1), 0)
     pick = jnp.where(srow // 8 == r_k, weight, 0.0)
@@ -235,7 +260,7 @@
         parts[pl.ds(pl.multiple_of(q * 16, 16), 16), :] = jnp.concatenate(outs, axis=0)
         return carry
 
-    lax.fori_loop(0, slots // 4, backward, 0, unroll=4)
+    lax.fori_loop(0, slots // 4, backward, 0, unroll=12)
 
     g_hi = spread[...].astype(jnp.bfloat16)
     for p in range(count):
@@ -260,10 +285,9 @@
     rows = count * days
     tiles = cells // 128
     own = rec // n
-    lists = block_lists.T
     vmem = pl.BlockSpec(memory_space=pltpu.VMEM)
     smem = pl.BlockSpec(memory_space=pltpu.SMEM)
-    hbm = pl.BlockSpec(memory_space=pl.ANY)
+    hbm = pl.BlockSpec(memory_space=pltpu.HBM)
     dma = pltpu.SemaphoreType.DMA
     hess, curv = pl.pallas_call(
         functools.partial(kernel, n),
@@ -271,9 +295,14 @@
             jax.ShapeDtypeStruct((rows, cells), jnp.float32),
             jax.ShapeDtypeStruct((count, 128), jnp.float32),
         ),
-        in_specs=[smem, smem, vmem, vmem, vmem, vmem, vmem, hbm, hbm],
+        in_specs=[smem, smem] + [hbm] * 6,
         out_specs=(vmem, vmem),
         scratch_shapes=[
+            pltpu.SMEM((3, slots), jnp.int32),
+            pltpu.VMEM((3, slots), jnp.int32),
+            pltpu.VMEM((slots,), jnp.float32),
+            pltpu.VMEM((1, cells), jnp.float32),
+            pltpu.VMEM((rec, 128), jnp.float32),
             pltpu.VMEM((rows, cells), jnp.float32),
             pltpu.VMEM((slots * 128, 128), jnp.bfloat16),
             pltpu.VMEM((tiles * rows + 2 * PAD, 128), jnp.float32),
@@ -283,7 +312,7 @@
             pltpu.VMEM((n, own, 8, 128), jnp.float32),
             pltpu.VMEM((n, own, 8, 128), jnp.float32),
             pltpu.VMEM((n, own, 8, 128), jnp.float32),
-            dma(()),
+            dma((6,)),
             dma((CHUNKS,)),
             dma((n,)),
             dma((n,)),
@@ -291,17 +320,16 @@
             dma((n,)),
         ],
         compiler_params=pltpu.CompilerParams(
-            collective_id=0, has_side_effects=True, vmem_limit_bytes=48 * 1024 * 1024
+            collective_id=0, has_side_effects=True, vmem_limit_bytes=LIMIT
         ),
     )(
-        lists,
         block_live,
-        corr_days.reshape(1, 1),
-        lists,
-        footprint_block_scale.reshape(1, slots),
-        prior_std.reshape(1, cells),
-        noise_inv.reshape(rec, 128),
-        probes.reshape(rows, cells),
+        corr_days,
+        hold(block_lists.T),
+        hold(footprint_block_scale),
+        hold(prior_std.reshape(1, cells)),
+        hold(noise_inv.reshape(rec, 128)),
+        hold(probes.reshape(rows, cells)),
         blocks.reshape(slots * 128, 128),
     )
     return hess.reshape(count, days, cells), curv[:, 0]

time: 31.3 us -> 26 us (0.83)
  local copies, waits for them, and re-layouts: 5.77 us -> 1.68 us
  Pallas kernels: 23.3 us -> 22.3 us
    unnamed x9 -> x1, local copies, waits for them, and re-layouts: 4.46 us -> 1.06 us
    pallas_call x1, Pallas kernels: 23.3 us -> 22.3 us  [shards(): pl.pallas_call(functools.partial(kernel, n), out_shape=(jax.ShapeDtypeStr...]
    reshape x1 -> x0, local copies, waits for them, and re-layouts: 0.68 us -> none  [shards(): footprint_block_scale.reshape(1, slots)]
where the time goes in v2:
time: 26 us; the launch traced here: 25.9 us
  Pallas kernels  22.3 us (86%)
  between operations  1.93 us (7%)
  local copies, waits for them, and re-layouts  1.68 us (6%)
    pallas_call x1, Pallas kernels, shards(): pl.pallas_call(functools.partial(kernel, n), out_shape=(jax.ShapeDtypeStr...  22.3 us
    unnamed x1, local copies, waits for them, and re-layouts  1.06 us
    slice x1, local copies, waits for them, and re-layouts, shards(): return (hess.reshape(count, days, cells), curv[:, 0])  0.63 us

profile of v2, /device:TPU:0, one launch (start us, length us, event | category | flops | bytes accessed | tf_op | source)
XLA Modules:
  0.0 25.9 jit_solution(3413730457426306753)
XLA Ops:
  1.9 22.3 %shard_map.95 = (f32[160,2048]{1,0:T(8,128)S(1)}, f32[4,128]{1,0:T(4,128)S(1)}) custom-call(s32[1]{0:T(128)S(6)} %copy.11.live_s, f32[1]{0:T(128)S(6)} %copy.12.corr_s, s32[3,288]{1,0:T(4,128)} %bitcast.11, f32[288]{0:T(512)} %scale_hbm.1, f32[1,2048]{1,0:T(1,128)} %bitcast.9, f32[16,128]{1,0:T(8,128)} %bitcast.10, f32[160,2048]{1,0:T(8,128)} %bitcast.8, ...), custom_call_target="tpu_custom_call" | custom-call | tf_op jit(solution)/shard_map/pallas_call | solution.py:292
  24.2 0.6 %slice_reduce_fusion = f32[4]{0:T(128)} fusion(f32[4,128]{1,0:T(4,128)S(1)} %get-tuple-element.5), kind=kLoop, calls=%fused_computation | loop fusion | bytes 32 | tf_op jit(solution)/shard_map/slice | solution.py:335
  24.8 1.1 %copy.13 = f32[4,40,2048]{2,1,0:T(8,128)} copy(f32[4,40,2048]{2,1,0:T(8,128)S(1)} %bitcast.6) | data formatting | bytes 2621440

commit v3 on v2

--- a/solution.py
+++ b/solution.py
@@ -8,7 +8,7 @@
 from jax.sharding import PartitionSpec as P
 
 MESH = pl.DeviceIdType.MESH
-CHUNKS = 8
+CHUNKS = 3
 PAD = 8
 LIMIT = 48 * 1024 * 1024
 
@@ -159,7 +159,7 @@
     quads = per // 4
     for c in range(CHUNKS):
         b_copies[c].wait()
-        lax.fori_loop(c * quads, (c + 1) * quads, forward, 0, unroll=9)
+        lax.fori_loop(c * quads, (c + 1) * quads, forward, 0, unroll=24)
 
     srow = lax.broadcasted_iota(jnp.int32, (rec * 8, 1), 0)
     pick = jnp.where(srow // 8 == r_k, weight, 0.0)
@@ -260,7 +260,7 @@
         parts[pl.ds(pl.multiple_of(q * 16, 16), 16), :] = jnp.concatenate(outs, axis=0)
         return carry
 
-    lax.fori_loop(0, slots // 4, backward, 0, unroll=12)
+    lax.fori_loop(0, slots // 4, backward, 0, unroll=24)
 
     g_hi = spread[...].astype(jnp.bfloat16)
     for p in range(count):

time: 26 us -> 24.5 us (0.942)
  Pallas kernels: 22.3 us -> 20.7 us
    pallas_call x1, Pallas kernels: 22.3 us -> 20.7 us  [shards(): pl.pallas_call(functools.partial(kernel, n), out_shape=(jax.ShapeDtypeStr...]
where the time goes in v3:
time: 24.5 us; the launch traced here: 24.3 us
  Pallas kernels  20.7 us (84%)
  between operations  1.93 us (8%)
  local copies, waits for them, and re-layouts  1.68 us (7%)
    pallas_call x1, Pallas kernels, shards(): pl.pallas_call(functools.partial(kernel, n), out_shape=(jax.ShapeDtypeStr...  20.7 us
    unnamed x1, local copies, waits for them, and re-layouts  1.06 us
    slice x1, local copies, waits for them, and re-layouts, shards(): return (hess.reshape(count, days, cells), curv[:, 0])  0.63 us

profile of v3, /device:TPU:0, one launch (start us, length us, event | category | flops | bytes accessed | tf_op | source)
XLA Modules:
  0.0 24.3 jit_solution(13494462501797510164)
XLA Ops:
  1.9 20.7 %shard_map.95 = (f32[160,2048]{1,0:T(8,128)S(1)}, f32[4,128]{1,0:T(4,128)S(1)}) custom-call(s32[1]{0:T(128)S(6)} %copy.11.live_s, f32[1]{0:T(128)S(6)} %copy.12.corr_s, s32[3,288]{1,0:T(4,128)} %bitcast.11, f32[288]{0:T(512)} %scale_hbm.1, f32[1,2048]{1,0:T(1,128)} %bitcast.9, f32[16,128]{1,0:T(8,128)} %bitcast.10, f32[160,2048]{1,0:T(8,128)} %bitcast.8, ...), custom_call_target="tpu_custom_call" | custom-call | tf_op jit(solution)/shard_map/pallas_call | solution.py:292
  22.6 0.6 %slice_reduce_fusion = f32[4]{0:T(128)} fusion(f32[4,128]{1,0:T(4,128)S(1)} %get-tuple-element.5), kind=kLoop, calls=%fused_computation | loop fusion | bytes 32 | tf_op jit(solution)/shard_map/slice | solution.py:335
  23.3 1.1 %copy.13 = f32[4,40,2048]{2,1,0:T(8,128)} copy(f32[4,40,2048]{2,1,0:T(8,128)S(1)} %bitcast.6) | data formatting | bytes 2621440

commit v4 on v3

--- a/solution.py
+++ b/solution.py
@@ -260,7 +260,7 @@
         parts[pl.ds(pl.multiple_of(q * 16, 16), 16), :] = jnp.concatenate(outs, axis=0)
         return carry
 
-    lax.fori_loop(0, slots // 4, backward, 0, unroll=24)
+    lax.fori_loop(0, slots // 4, backward, 0, unroll=36)
 
     g_hi = spread[...].astype(jnp.bfloat16)
     for p in range(count):

time: 24.5 us -> 24.4 us (level)
  no operation moved by 1% of the time
where the time goes in v4:
time: 24.4 us; the launch traced here: 24.2 us
  Pallas kernels  20.6 us (84%)
  between operations  1.93 us (8%)
  local copies, waits for them, and re-layouts  1.68 us (7%)
    pallas_call x1, Pallas kernels, shards(): pl.pallas_call(functools.partial(kernel, n), out_shape=(jax.ShapeDtypeStr...  20.6 us
    unnamed x1, local copies, waits for them, and re-layouts  1.06 us
    slice x1, local copies, waits for them, and re-layouts, shards(): return (hess.reshape(count, days, cells), curv[:, 0])  0.63 us

profile of v4, /device:TPU:0, one launch (start us, length us, event | category | flops | bytes accessed | tf_op | source)
XLA Modules:
  0.0 24.2 jit_solution(16463849840095798630)
XLA Ops:
  1.9 20.6 %shard_map.95 = (f32[160,2048]{1,0:T(8,128)S(1)}, f32[4,128]{1,0:T(4,128)S(1)}) custom-call(s32[1]{0:T(128)S(6)} %copy.11.live_s, f32[1]{0:T(128)S(6)} %copy.12.corr_s, s32[3,288]{1,0:T(4,128)} %bitcast.11, f32[288]{0:T(512)} %scale_hbm.1, f32[1,2048]{1,0:T(1,128)} %bitcast.9, f32[16,128]{1,0:T(8,128)} %bitcast.10, f32[160,2048]{1,0:T(8,128)} %bitcast.8, ...), custom_call_target="tpu_custom_call" | custom-call | tf_op jit(solution)/shard_map/pallas_call | solution.py:292
  22.5 0.6 %slice_reduce_fusion = f32[4]{0:T(128)} fusion(f32[4,128]{1,0:T(4,128)S(1)} %get-tuple-element.5), kind=kLoop, calls=%fused_computation | loop fusion | bytes 32 | tf_op jit(solution)/shard_map/slice | solution.py:335
  23.2 1.1 %copy.13 = f32[4,40,2048]{2,1,0:T(8,128)} copy(f32[4,40,2048]{2,1,0:T(8,128)S(1)} %bitcast.6) | data formatting | bytes 2621440
